TPU v7x, 32 devices: a whole 2x2x4 slice. The times are simulated.
32 devices in a mesh: row: 4 (over y, x), col: 4 (over z), rep: 2 (over core).
Axes of the slice: x: 2, y: 2, z: 4, core: 2. Of those that a mesh axis runs over, the one named last changes fastest.
Arguments:
- features: bfloat16 [2, 2048, 512], P('rep', ('row', 'col')), may hold values from -6 to 6
- cotangent: bfloat16 [2, 2048, 512], P('rep', ('row', 'col')), may hold values from -6 to 6
- weight: bfloat16 [512, 512], replicated, may hold values from -0.25 to 0.25
- tile_values: bfloat16 [2, 256, 128, 128], P('rep', ('row', 'col')), may hold values from -0.25 to 0.25
- tile_out: int32 [2, 256], P('rep', ('row', 'col')), may hold values from 0 to 3
- tile_in: int32 [2, 256], P('rep', ('row', 'col')), may hold values from 0 to 3
- tile_count: int32 [2, 16], P('rep', ('row', 'col')), may hold values from 8 to 16, as said below
Outputs:
- out_feats: bfloat16 [2, 2048, 512], P('rep', ('row', 'col'))
- grad_feats: bfloat16 [2, 2048, 512], P('rep', ('row', 'col'))
- grad_weight: float32 [512, 512], replicated
Inputs may be any that keep to these rules, and one draw needn't show every extreme that they name: `tile_count`: in each window some group has all 16 slots live.
All inputs are finite; a program needn't handle non-finite values.
Results may differ from a plain program's by a relative error of at most 0.015.
Values may be sent and summed in bfloat16 or wider, within the bound.
A program may use at most 64 MiB of HBM per device.

v0:
```python
import jax
import jax.numpy as jnp
from jax import lax
from jax.sharding import PartitionSpec as P

SECTIONS = 4


def passed_along(value, axis, steps):
    count = lax.axis_size(axis)
    leading, last = (max(0, -steps), min(count, count - steps))
    return lax.ppermute(value, axis, [(source, source + steps) for source in range(leading, last)])


def body(features, cotangent, weight, tile_values, tile_out, tile_in, tile_count):
    field_in = features[0]
    values = tile_values[0]
    outs_idx = tile_out[0]
    ins_idx = tile_in[0]
    count = tile_count[0, 0]
    node_rows, width = field_in.shape
    edge = values.shape[-1]
    per_span = node_rows // edge
    half = SECTIONS // 2
    col_count = lax.axis_size("col")
    out_count = col_count * per_span
    in_count = SECTIONS * per_span
    slot_total = values.shape[0]
    live = (jnp.arange(slot_total, dtype=jnp.int32) < count).astype(jnp.float32)
    out_hot = (outs_idx[None, :] == jnp.arange(out_count, dtype=jnp.int32)[:, None]).astype(
        jnp.float32
    ) * live[None, :]
    in_hot = (ins_idx[None, :] == jnp.arange(in_count, dtype=jnp.int32)[:, None]).astype(
        jnp.float32
    ) * live[None, :]
    pieces = []
    for section in range(SECTIONS):
        offset = section - half
        if offset == 0:
            pieces.append(field_in)
        else:
            pieces.append(passed_along(field_in, "row", -offset))
    blocks = jnp.stack(pieces)
    picked = blocks[ins_idx]
    prods = jnp.einsum("tij,tjf->tif", values, picked, preferred_element_type=jnp.float32)
    part = jnp.einsum("ot,tif->oif", out_hot, prods, precision=lax.Precision.HIGHEST)
    summed = lax.psum_scatter(
        part.reshape(out_count * edge, width).astype(jnp.bfloat16),
        "col",
        scatter_dimension=0,
        tiled=True,
    )
    pre = jnp.dot(summed, weight, preferred_element_type=jnp.float32)
    out_feats = jax.nn.silu(pre).astype(jnp.bfloat16)
    sigma = jax.nn.sigmoid(pre)
    dpre = (cotangent[0].astype(jnp.float32) * sigma * (1.0 + pre * (1.0 - sigma))).astype(
        jnp.bfloat16
    )
    local_grad = jnp.einsum("nf,ng->fg", summed, dpre, preferred_element_type=jnp.float32)
    total_nodes = node_rows * lax.axis_size("row") * col_count * lax.axis_size("rep")
    grad_weight = lax.psum(local_grad, ("row", "col", "rep")) * jnp.float32(total_nodes) ** (-0.5)
    dhidden = jnp.einsum("nf,gf->ng", dpre, weight, preferred_element_type=jnp.float32).astype(
        jnp.bfloat16
    )
    row_grads = lax.all_gather(dhidden, "col", axis=0, tiled=True).reshape(out_count, edge, width)
    chosen = row_grads[outs_idx]
    back_prods = jnp.einsum("tij,tif->tjf", values, chosen, preferred_element_type=jnp.float32)
    sections_part = jnp.einsum("it,tjf->ijf", in_hot, back_prods, precision=lax.Precision.HIGHEST)
    sections_part = sections_part.astype(jnp.bfloat16)
    total = jnp.zeros((node_rows, width), jnp.float32)
    for section in range(SECTIONS):
        offset = section - half
        if offset == 0:
            arrived = sections_part[section]
        else:
            arrived = passed_along(sections_part[section], "row", offset)
        total = total + arrived.astype(jnp.float32)
    grad_feats = total.astype(jnp.bfloat16)
    return (out_feats[None], grad_feats[None], grad_weight)


def solution(mesh):
    return jax.shard_map(
        body,
        mesh=mesh,
        in_specs=(
            P("rep", ("row", "col"), None),
            P("rep", ("row", "col"), None),
            P(),
            P("rep", ("row", "col"), None, None),
            P("rep", ("row", "col")),
            P("rep", ("row", "col")),
            P("rep", ("row", "col")),
        ),
        out_specs=(P("rep", ("row", "col"), None), P("rep", ("row", "col"), None), P()),
        check_vma=False,
    )
```

profile of v0, /device:TPU:0, one launch (start us, length us, event | category | flops | bytes accessed | tf_op | source)
XLA Modules:
  0.0 224.5 jit_solution(10835809086337116893)
XLA Ops:
  7.2 5.0 %collective-permute-start = (bf16[128,512]{1,0:T(8,128)(2,1)}, bf16[128,512]{1,0:T(8,128)(2,1)S(1)}, u32[]{:S(2)}, u32[]{:S(2)}) collective-permute-start(bf16[128,512]{1,0:T(8,128)(2,1)} %bitcast.76), channel_id=1, source_target_pairs={{0,16},{8,24},{1,17},{9,25},{2,18},{10,26},{3,19},{11,27},{4,20},{... | collective-permute-start | bytes 393224 | tf_op jit(solution)/shard_map/ppermute | solution.py:12
  12.2 3.4 %collective-permute-start.1 = (bf16[128,512]{1,0:T(8,128)(2,1)}, bf16[128,512]{1,0:T(8,128)(2,1)S(1)}, u32[]{:S(2)}, u32[]{:S(2)}) collective-permute-start(bf16[128,512]{1,0:T(8,128)(2,1)} %bitcast.77), channel_id=1, source_target_pairs={{0,8},{8,16},{16,24},{1,9},{9,17},{17,25},{2,10},{10,18},{18,26},{... | collective-permute-start | bytes 393224 | tf_op jit(solution)/shard_map/ppermute | solution.py:12
  15.7 1.3 collective-permute-start.2
  17.0 0.7 fusion.30
  18.3 0.2 collective-permute-done.1
  18.5 4.3 %collective-permute-done.2 = bf16[128,512]{1,0:T(8,128)(2,1)S(1)} collective-permute-done((bf16[128,512]{1,0:T(8,128)(2,1)}, bf16[128,512]{1,0:T(8,128)(2,1)S(1)}, u32[]{:S(2)}, u32[]{:S(2)}) %collective-permute-start.2) | collective-permute-done | bytes 131104 | tf_op jit(solution)/shard_map/ppermute | solution.py:12
  22.7 1.0 pad_maximum_fusion
  23.7 0.7 gather_fusion
  24.4 2.7 %fusion.12 = f32[16,512,128]{2,1,0:T(8,128)} fusion(bf16[16,128,512]{2,1,0:T(8,128)(2,1)S(1)} %gather_fusion, bf16[1,16,128,128]{3,2,1,0:T(8,128)(2,1)S(1)} %copy-done), kind=kOutput, calls=%fused_computation.12 | convolution fusion | flops 268435456 | bytes 6815744 | tf_op jit(solution)/shard_map/tij,tjf->tif/dot_general | solution.py:45
  27.1 5.5 %copy.16 = f32[16,512,128]{1,0,2:T(8,128)} copy(f32[16,512,128]{2,1,0:T(8,128)} %fusion.12) | data formatting | bytes 8388608 | tf_op jit(solution)/shard_map/tij,tjf->tif/dot_general | solution.py:45
  32.6 4.3 %fusion.4 = bf16[4,128,512]{2,0,1:T(4,128)(2,1)S(1)} fusion(f32[16,512,128]{1,0,2:T(8,128)} %copy.16, f32[16]{0:T(128)S(1)} %compare_convert_fusion, s32[16]{0:T(128)S(1)} %bitcast.82), kind=kOutput, calls=%fused_computation.6 | convolution fusion | flops 50593920 | bytes 4718720 | tf_op jit(solution)/shard_map/ot,tif->oif/dot_general | solution.py:46
  37.0 0.9 copy.13
  37.9 0.0 all-reduce.2.cloned.1.call-start
  38.0 21.4 %reduce-scatter.2.cloned.1.call-done = bf16[128,512]{1,0:T(8,128)(2,1)} async-done(((bf16[512,512]{1,0:T(8,128)(2,1)}), bf16[128,512]{1,0:T(8,128)(2,1)}) %reduce-scatter.2.cloned.1.call-update) | async-done | bytes 131088 | tf_op jit(solution)/shard_map/reduce_scatter | solution.py:47
  59.4 1.1 fusion.38
  60.6 0.3 convolution_convert_fusion
  60.9 15.9 %all_gather.3 = bf16[512,512]{1,0:T(8,128)(2,1)S(1)} all-gather(bf16[128,512]{1,0:T(8,128)(2,1)S(1)} %convolution_convert_fusion), channel_id=1, replica_groups=mesh['row'=4,'col'=4,'rep'=2] {'col'}, dimensions={0}, use_global_device_ids=true | all-gather | bytes 655360 | tf_op jit(solution)/shard_map/all_gather | solution.py:65
  76.7 0.7 gather_fusion.1
  77.4 2.8 %fusion.10 = f32[16,512,128]{2,1,0:T(8,128)} fusion(bf16[16,128,512]{2,1,0:T(8,128)(2,1)S(1)} %gather_fusion.1, bf16[1,16,128,128]{3,2,1,0:T(8,128)(2,1)S(1)} %copy-done), kind=kOutput, calls=%fused_computation.10 | convolution fusion | flops 268435456 | bytes 6815744 | tf_op jit(solution)/shard_map/tij,tif->tjf/dot_general | solution.py:67
  80.2 5.5 %copy.17 = f32[16,512,128]{1,0,2:T(8,128)} copy(f32[16,512,128]{2,1,0:T(8,128)} %fusion.10) | data formatting | bytes 8388608 | tf_op jit(solution)/shard_map/tij,tif->tjf/dot_general | solution.py:67
  85.7 1.4 fusion.34
  87.1 4.3 %fusion.7 = bf16[4,128,512]{2,0,1:T(4,128)(2,1)S(1)} fusion(f32[16,512,128]{1,0,2:T(8,128)} %copy.17, s32[16]{0:T(128)S(1)} %bitcast.83, f32[16]{0:T(128)S(1)} %compare_convert_fusion), kind=kOutput, calls=%fused_computation.7 | convolution fusion | flops 50593920 | bytes 4718720 | tf_op jit(solution)/shard_map/it,tjf->ijf/dot_general | solution.py:68
  91.4 0.7 fusion.37
  92.1 1.3 collective-permute-start.3
  93.5 1.3 collective-permute-start.4
  94.8 4.6 %collective-permute-start.5 = (bf16[128,512]{1,0:T(8,128)(2,1)S(1)}, bf16[128,512]{1,0:T(8,128)(2,1)S(1)}, u32[]{:S(2)}, u32[]{:S(2)}) collective-permute-start(bf16[128,512]{1,0:T(8,128)(2,1)S(1)} %bitcast.75), channel_id=1, source_target_pairs={{0,8},{8,16},{16,24},{1,9},{9,17},{17,25},{2,10},{10,18},{18,26},{... | collective-permute-start | bytes 393224 | tf_op jit(solution)/shard_map/ppermute | solution.py:12
  99.4 0.7 fusion.19
  100.1 0.2 collective-permute-done.4
  100.3 1.7 collective-permute-done.5
  102.0 0.7 fusion.18
  102.7 112.6 %all-reduce.2.cloned.1.call-done = f32[512,512]{1,0:T(8,128)} async-done(((f32[512,512]{1,0:T(8,128)}), f32[512,512]{1,0:T(8,128)}) %all-reduce.2.cloned.1.call-update) | async-done | bytes 1048592 | tf_op jit(solution)/shard_map/psum | solution.py:61
  215.3 2.3 %broadcast_multiply_fusion = f32[512,512]{1,0:T(8,128)} fusion(f32[512,512]{1,0:T(8,128)} %all-reduce.2.cloned.1.call-done), kind=kLoop, calls=%fused_computation.14 | loop fusion | flops 262144 | bytes 2097152 | tf_op jit(solution)/shard_map/mul | solution.py:61
  (24 shorter events, 0.2 us)
Async XLA Ops:
  7.2 17.2 %copy-start = (bf16[1,16,128,128]{3,2,1,0:T(8,128)(2,1)S(1)}, bf16[1,16,128,128]{3,2,1,0:T(8,128)(2,1)}, u32[]{:S(2)}) copy-start(bf16[1,16,128,128]{3,2,1,0:T(8,128)(2,1)} %param.10) | copy-start | bytes 1572868
  7.2 52.2 %reduce-scatter.2.cloned.1.call-start = ((), (), s32[]{:S(2)}) async-start(), calls=%async_computation.1 | async-start | bytes 655360 | tf_op jit(solution)/shard_map/reduce_scatter | solution.py:47
  7.2 11.1 %collective-permute-start = (bf16[128,512]{1,0:T(8,128)(2,1)}, bf16[128,512]{1,0:T(8,128)(2,1)S(1)}, u32[]{:S(2)}, u32[]{:S(2)}) collective-permute-start(bf16[128,512]{1,0:T(8,128)(2,1)} %bitcast.76), channel_id=1, source_target_pairs={{0,16},{8,24},{1,17},{9,25},{2,18},{10,26},{3,19},{11,27},{4,20},{... | collective-permute-start | bytes 393224 | tf_op jit(solution)/shard_map/ppermute | solution.py:12
  12.2 6.2 %collective-permute-start.1 = (bf16[128,512]{1,0:T(8,128)(2,1)}, bf16[128,512]{1,0:T(8,128)(2,1)S(1)}, u32[]{:S(2)}, u32[]{:S(2)}) collective-permute-start(bf16[128,512]{1,0:T(8,128)(2,1)} %bitcast.77), channel_id=1, source_target_pairs={{0,8},{8,16},{16,24},{1,9},{9,17},{17,25},{2,10},{10,18},{18,26},{... | collective-permute-start | bytes 393224 | tf_op jit(solution)/shard_map/ppermute | solution.py:12
  15.7 7.1 %collective-permute-start.2 = (bf16[128,512]{1,0:T(8,128)(2,1)}, bf16[128,512]{1,0:T(8,128)(2,1)S(1)}, u32[]{:S(2)}, u32[]{:S(2)}) collective-permute-start(bf16[128,512]{1,0:T(8,128)(2,1)} %bitcast.78), channel_id=1, source_target_pairs={{8,0},{16,8},{24,16},{9,1},{17,9},{25,17},{10,2},{18,10},{26,18},{... | collective-permute-start | bytes 393224 | tf_op jit(solution)/shard_map/ppermute | solution.py:12
  27.1 5.5 %copy-start.3 = (s32[1,16]{1,0:T(1,128)S(1)}, s32[1,16]{1,0:T(1,128)}, u32[]{:S(2)}) copy-start(s32[1,16]{1,0:T(1,128)} %param.11) | copy-start | bytes 196
  32.6 26.8 %copy-start.1 = (bf16[512,512]{1,0:T(8,128)(2,1)S(1)}, bf16[512,512]{1,0:T(8,128)(2,1)}, u32[]{:S(2)}) copy-start(bf16[512,512]{1,0:T(8,128)(2,1)} %param.9) | copy-start | bytes 1572868
  37.0 23.6 %copy-start.5 = (bf16[1,128,512]{2,1,0:T(8,128)(2,1)S(1)}, bf16[1,128,512]{2,1,0:T(8,128)(2,1)}, u32[]{:S(2)}) copy-start(bf16[1,128,512]{2,1,0:T(8,128)(2,1)} %param.8) | copy-start | bytes 393220
  37.9 177.4 %all-reduce.2.cloned.1.call-start = ((), (), s32[]{:S(2)}) async-start(), calls=%async_computation.2 | async-start | bytes 2097152 | tf_op jit(solution)/shard_map/psum | solution.py:61
  80.2 5.5 %copy-start.2 = (bf16[128,512]{1,0:T(8,128)(2,1)S(1)}, bf16[128,512]{1,0:T(8,128)(2,1)}, u32[]{:S(2)}) copy-start(bf16[128,512]{1,0:T(8,128)(2,1)} %reduce-scatter.2.cloned.1.call-done) | copy-start | bytes 393220
  85.7 1.4 copy-start.4
  92.1 8.0 %collective-permute-start.3 = (bf16[128,512]{1,0:T(8,128)(2,1)S(1)}, bf16[128,512]{1,0:T(8,128)(2,1)S(1)}, u32[]{:S(2)}, u32[]{:S(2)}) collective-permute-start(bf16[128,512]{1,0:T(8,128)(2,1)S(1)} %bitcast.73), channel_id=1, source_target_pairs={{16,0},{24,8},{17,1},{25,9},{18,2},{26,10},{19,3},{27,11},{20,4},{... | collective-permute-start | bytes 393224 | tf_op jit(solution)/shard_map/ppermute | solution.py:12
  93.5 6.9 %collective-permute-start.4 = (bf16[128,512]{1,0:T(8,128)(2,1)S(1)}, bf16[128,512]{1,0:T(8,128)(2,1)S(1)}, u32[]{:S(2)}, u32[]{:S(2)}) collective-permute-start(bf16[128,512]{1,0:T(8,128)(2,1)S(1)} %bitcast.74), channel_id=1, source_target_pairs={{8,0},{16,8},{24,16},{9,1},{17,9},{25,17},{10,2},{18,10},{26,18},{... | collective-permute-start | bytes 393224 | tf_op jit(solution)/shard_map/ppermute | solution.py:12
  94.8 7.2 %collective-permute-start.5 = (bf16[128,512]{1,0:T(8,128)(2,1)S(1)}, bf16[128,512]{1,0:T(8,128)(2,1)S(1)}, u32[]{:S(2)}, u32[]{:S(2)}) collective-permute-start(bf16[128,512]{1,0:T(8,128)(2,1)S(1)} %bitcast.75), channel_id=1, source_target_pairs={{0,8},{8,16},{16,24},{1,9},{9,17},{17,25},{2,10},{10,18},{18,26},{... | collective-permute-start | bytes 393224 | tf_op jit(solution)/shard_map/ppermute | solution.py:12
Sparse Core Ops, SparseCore 0:
  38.0 21.3 reduce-scatter.1
  87.2 128.0 all-reduce.1
where the time goes:
time: 225 us; the launch traced here: 224 us
  waiting for transfers between devices  140 us (62%)
  starting transfers between devices  16.9 us (8%)
  matrix products  16.9 us (8%)
  blocking collectives  15.9 us (7%)
  between operations  14.9 us (7%)
  local copies, waits for them, and re-layouts  13.4 us (6%)
  other arithmetic  6.11 us (3%)
    psum x1, waiting for transfers between devices, body(): lax.psum(local_grad, ('row', 'col', 'rep'))  113 us
    reduce_scatter x1, waiting for transfers between devices, body(): lax.psum_scatter(part.reshape(out_count * edge, width).astype(jnp.bfloat1...  21.4 us
    ppermute x6, starting transfers between devices, passed_along(): lax.ppermute(value, axis, [(source, source + steps) for source in range(l...  16.8 us
    all_gather x1, blocking collectives, body(): lax.all_gather(dhidden, 'col', axis=0, tiled=True)  15.9 us
    ppermute x6, waiting for transfers between devices, passed_along(): lax.ppermute(value, axis, [(source, source + steps) for source in range(l...  6.33 us
    dot_general x1, local copies, waits for them, and re-layouts, body(): jnp.einsum('tij,tif->tjf', values, chosen, preferred_element_type=jnp.flo...  5.54 us
    dot_general x1, local copies, waits for them, and re-layouts, body(): jnp.einsum('tij,tjf->tif', values, picked, preferred_element_type=jnp.flo...  5.51 us
  transfers between devices with their start and end apart: 8, of which 6 were waited for; matrix products, arithmetic and copies ran while one was open for 3% of the time, Pallas kernels for 0%

commit v1 on v0

--- a/solution.py
+++ b/solution.py
@@ -4,6 +4,24 @@
 from jax.sharding import PartitionSpec as P
 
 SECTIONS = 4
+
+
+def gather_around(shard, axis, dim):
+    ways, here, step = (lax.axis_size(axis), lax.axis_index(axis), shard.shape[dim])
+    shape = [n * ways if d == dim else n for d, n in enumerate(shard.shape)]
+    full = lax.dynamic_update_slice_in_dim(
+        jnp.zeros(shape, shard.dtype), shard, here * step, axis=dim
+    )
+    going_up = going_down = shard
+    for far in range(1, ways // 2 + 1):
+        going_up = lax.ppermute(going_up, axis, [(d, (d + 1) % ways) for d in range(ways)])
+        full = lax.dynamic_update_slice_in_dim(full, going_up, (here - far) % ways * step, axis=dim)
+        if 2 * far < ways:
+            going_down = lax.ppermute(going_down, axis, [(d, (d - 1) % ways) for d in range(ways)])
+            full = lax.dynamic_update_slice_in_dim(
+                full, going_down, (here + far) % ways * step, axis=dim
+            )
+    return full
 
 
 def passed_along(value, axis, steps):
@@ -62,7 +80,7 @@
     dhidden = jnp.einsum("nf,gf->ng", dpre, weight, preferred_element_type=jnp.float32).astype(
         jnp.bfloat16
     )
-    row_grads = lax.all_gather(dhidden, "col", axis=0, tiled=True).reshape(out_count, edge, width)
+    row_grads = gather_around(dhidden, "col", 0).reshape(out_count, edge, width)
     chosen = row_grads[outs_idx]
     back_prods = jnp.einsum("tij,tif->tjf", values, chosen, preferred_element_type=jnp.float32)
     sections_part = jnp.einsum("it,tjf->ijf", in_hot, back_prods, precision=lax.Precision.HIGHEST)

time: 225 us -> 204 us (0.907)
  blocking collectives: 15.9 us -> 0 us
  waiting for transfers between devices: 140 us -> 132 us
  starting transfers between devices: 16.9 us -> 20.8 us
    psum x1, waiting for transfers between devices: 113 us -> 94.2 us  [body(): lax.psum(local_grad, ('row', 'col', 'rep'))]
    all_gather x1 -> x0, blocking collectives: 15.9 us -> none  [body(): lax.all_gather(dhidden, 'col', axis=0, tiled=True)]
    ppermute x0 -> x3, waiting for transfers between devices: none -> 9.13 us  [the longest x2 9.13 us: gather_around(): lax.ppermute(going_up, axis, [(d, (d + 1) % ways) for d in range(ways)])]
    ppermute x0 -> x3, starting transfers between devices: none -> 3.87 us  [the longest x1 3.81 us: gather_around(): lax.ppermute(going_down, axis, [(d, (d - 1) % ways) for d in range(ways)])]
  transfers between devices with their start and end apart: 8 -> 11, of which waited for: 6 -> 8; matrix products, arithmetic and copies ran while one was open for 3% -> 9% of each run, Pallas kernels for 0% -> 0%
where the time goes in v1:
time: 204 us
  waiting for transfers between devices  132 us (65%)
  starting transfers between devices  20.8 us (10%)
  matrix products  17 us (8%)
  between operations  15 us (7%)
  local copies, waits for them, and re-layouts  13.5 us (7%)
  other arithmetic  6.11 us (3%)
    psum x1, waiting for transfers between devices, body(): lax.psum(local_grad, ('row', 'col', 'rep'))  94.2 us
    reduce_scatter x1, waiting for transfers between devices, body(): lax.psum_scatter(part.reshape(out_count * edge, width).astype(jnp.bfloat1...  21.4 us
    ppermute x6, starting transfers between devices, passed_along(): lax.ppermute(value, axis, [(source, source + steps) for source in range(l...  16.8 us
    ppermute x2, waiting for transfers between devices, gather_around(): lax.ppermute(going_up, axis, [(d, (d + 1) % ways) for d in range(ways)])  9.13 us
    ppermute x6, waiting for transfers between devices, passed_along(): lax.ppermute(value, axis, [(source, source + steps) for source in range(l...  6.86 us
    dot_general x1, local copies, waits for them, and re-layouts, body(): jnp.einsum('tij,tif->tjf', values, chosen, preferred_element_type=jnp.flo...  5.52 us
    dot_general x1, local copies, waits for them, and re-layouts, body(): jnp.einsum('tij,tjf->tif', values, picked, preferred_element_type=jnp.flo...  5.51 us
    dot_general x1, matrix products, body(): jnp.einsum('ot,tif->oif', out_hot, prods, precision=lax.Precision.HIGHEST)  4.33 us
  transfers between devices with their start and end apart: 11, of which 8 were waited for; matrix products, arithmetic and copies ran while one was open for 9% of the time, Pallas kernels for 0%

profile of v1, /device:TPU:0, one launch (start us, length us, event | category | flops | bytes accessed | tf_op | source)
XLA Modules:
  0.0 203.9 jit_solution(7871122721037286208)
XLA Ops:
  7.2 5.0 %collective-permute-start = (bf16[128,512]{1,0:T(8,128)(2,1)}, bf16[128,512]{1,0:T(8,128)(2,1)S(1)}, u32[]{:S(2)}, u32[]{:S(2)}) collective-permute-start(bf16[128,512]{1,0:T(8,128)(2,1)} %bitcast.78), channel_id=1, source_target_pairs={{0,16},{8,24},{1,17},{9,25},{2,18},{10,26},{3,19},{11,27},{4,20},{... | collective-permute-start | bytes 393224 | tf_op jit(solution)/shard_map/ppermute | solution.py:30
  12.2 3.4 %collective-permute-start.1 = (bf16[128,512]{1,0:T(8,128)(2,1)}, bf16[128,512]{1,0:T(8,128)(2,1)S(1)}, u32[]{:S(2)}, u32[]{:S(2)}) collective-permute-start(bf16[128,512]{1,0:T(8,128)(2,1)} %bitcast.79), channel_id=1, source_target_pairs={{0,8},{8,16},{16,24},{1,9},{9,17},{17,25},{2,10},{10,18},{18,26},{... | collective-permute-start | bytes 393224 | tf_op jit(solution)/shard_map/ppermute | solution.py:30
  15.7 1.3 collective-permute-start.2
  17.0 0.7 fusion.30
  18.5 4.3 %collective-permute-done.2 = bf16[128,512]{1,0:T(8,128)(2,1)S(1)} collective-permute-done((bf16[128,512]{1,0:T(8,128)(2,1)}, bf16[128,512]{1,0:T(8,128)(2,1)S(1)}, u32[]{:S(2)}, u32[]{:S(2)}) %collective-permute-start.2) | collective-permute-done | bytes 131104 | tf_op jit(solution)/shard_map/ppermute | solution.py:30
  22.7 1.0 pad_maximum_fusion
  23.7 0.7 gather_fusion
  24.4 2.7 %fusion.12 = f32[16,512,128]{2,1,0:T(8,128)} fusion(bf16[16,128,512]{2,1,0:T(8,128)(2,1)S(1)} %gather_fusion, bf16[1,16,128,128]{3,2,1,0:T(8,128)(2,1)S(1)} %copy-done), kind=kOutput, calls=%fused_computation.12 | convolution fusion | flops 268435456 | bytes 6815744 | tf_op jit(solution)/shard_map/tij,tjf->tif/dot_general | solution.py:63
  27.1 5.5 %copy.16 = f32[16,512,128]{1,0,2:T(8,128)} copy(f32[16,512,128]{2,1,0:T(8,128)} %fusion.12) | data formatting | bytes 8388608 | tf_op jit(solution)/shard_map/tij,tjf->tif/dot_general | solution.py:63
  32.7 4.3 %fusion.4 = bf16[4,128,512]{2,0,1:T(4,128)(2,1)S(1)} fusion(f32[16,512,128]{1,0,2:T(8,128)} %copy.16, f32[16]{0:T(128)S(1)} %compare_convert_fusion, s32[16]{0:T(128)S(1)} %bitcast.84), kind=kOutput, calls=%fused_computation.6 | convolution fusion | flops 50593920 | bytes 4718720 | tf_op jit(solution)/shard_map/ot,tif->oif/dot_general | solution.py:64
  37.0 0.9 copy.13
  38.1 21.4 %reduce-scatter.2.cloned.1.call-done = bf16[128,512]{1,0:T(8,128)(2,1)} async-done(((bf16[512,512]{1,0:T(8,128)(2,1)}), bf16[128,512]{1,0:T(8,128)(2,1)}) %reduce-scatter.2.cloned.1.call-update) | async-done | bytes 131088 | tf_op jit(solution)/shard_map/reduce_scatter | solution.py:65
  59.5 1.2 fusion.38
  60.7 0.3 constant_dynamic-update-slice_fusion.3
  61.1 3.8 %collective-permute-start.4 = (bf16[128,512]{1,0:T(8,128)(2,1)S(1)}, bf16[128,512]{1,0:T(8,128)(2,1)S(1)}, u32[]{:S(2)}, u32[]{:S(2)}) collective-permute-start(bf16[128,512]{1,0:T(8,128)(2,1)S(1)} %get-tuple-element.8), channel_id=1, source_target_pairs={{0,6},{2,0},{4,2},{6,4},{1,7},{3,1},{5,3},{7,5},{8,14},{10,8},{12,... | collective-permute-start | bytes 393224 | tf_op jit(solution)/shard_map/ppermute | solution.py:20
  64.9 1.3 fusion.34
  66.3 1.7 collective-permute-done.3
  68.0 7.5 %collective-permute-done.5 = bf16[128,512]{1,0:T(8,128)(2,1)S(1)} collective-permute-done((bf16[128,512]{1,0:T(8,128)(2,1)S(1)}, bf16[128,512]{1,0:T(8,128)(2,1)S(1)}, u32[]{:S(2)}, u32[]{:S(2)}) %collective-permute-start.5) | collective-permute-done | bytes 131104 | tf_op jit(solution)/shard_map/ppermute | solution.py:17
  75.5 0.7 gather_fusion.1
  76.2 2.7 %fusion.10 = f32[16,512,128]{2,1,0:T(8,128)} fusion(bf16[16,128,512]{2,1,0:T(8,128)(2,1)S(1)} %gather_fusion.1, bf16[1,16,128,128]{3,2,1,0:T(8,128)(2,1)S(1)} %copy-done), kind=kOutput, calls=%fused_computation.10 | convolution fusion | flops 268435456 | bytes 6815744 | tf_op jit(solution)/shard_map/tij,tif->tjf/dot_general | solution.py:85
  78.9 5.5 %copy.17 = f32[16,512,128]{1,0,2:T(8,128)} copy(f32[16,512,128]{2,1,0:T(8,128)} %fusion.10) | data formatting | bytes 8388608 | tf_op jit(solution)/shard_map/tij,tif->tjf/dot_general | solution.py:85
  84.4 4.3 %fusion.7 = bf16[4,128,512]{2,0,1:T(4,128)(2,1)S(1)} fusion(f32[16,512,128]{1,0,2:T(8,128)} %copy.17, s32[16]{0:T(128)S(1)} %bitcast.85, f32[16]{0:T(128)S(1)} %compare_convert_fusion), kind=kOutput, calls=%fused_computation.7 | convolution fusion | flops 50593920 | bytes 4718720 | tf_op jit(solution)/shard_map/it,tjf->ijf/dot_general | solution.py:86
  88.7 0.7 fusion.37
  89.5 1.3 collective-permute-start.6
  90.8 1.3 collective-permute-start.7
  92.2 4.6 %collective-permute-start.8 = (bf16[128,512]{1,0:T(8,128)(2,1)S(1)}, bf16[128,512]{1,0:T(8,128)(2,1)S(1)}, u32[]{:S(2)}, u32[]{:S(2)}) collective-permute-start(bf16[128,512]{1,0:T(8,128)(2,1)S(1)} %bitcast.77), channel_id=1, source_target_pairs={{0,8},{8,16},{16,24},{1,9},{9,17},{17,25},{2,10},{10,18},{18,26},{... | collective-permute-start | bytes 393224 | tf_op jit(solution)/shard_map/ppermute | solution.py:30
  96.7 0.7 fusion.19
  97.5 0.2 collective-permute-done.7
  97.7 2.2 %collective-permute-done.8 = bf16[128,512]{1,0:T(8,128)(2,1)S(1)} collective-permute-done((bf16[128,512]{1,0:T(8,128)(2,1)S(1)}, bf16[128,512]{1,0:T(8,128)(2,1)S(1)}, u32[]{:S(2)}, u32[]{:S(2)}) %collective-permute-start.8) | collective-permute-done | bytes 131104 | tf_op jit(solution)/shard_map/ppermute | solution.py:30
  99.9 0.7 fusion.18
  100.6 94.2 %all-reduce.2.cloned.1.call-done = f32[512,512]{1,0:T(8,128)} async-done(((f32[512,512]{1,0:T(8,128)}), f32[512,512]{1,0:T(8,128)}) %all-reduce.2.cloned.1.call-update) | async-done | bytes 1048592 | tf_op jit(solution)/shard_map/psum | solution.py:79
  194.8 2.3 %broadcast_multiply_fusion = f32[512,512]{1,0:T(8,128)} fusion(f32[512,512]{1,0:T(8,128)} %all-reduce.2.cloned.1.call-done), kind=kLoop, calls=%fused_computation.14 | loop fusion | flops 262144 | bytes 2097152 | tf_op jit(solution)/shard_map/mul | solution.py:79
  (33 shorter events, 0.5 us)
Async XLA Ops:
  7.2 17.2 %copy-start = (bf16[1,16,128,128]{3,2,1,0:T(8,128)(2,1)S(1)}, bf16[1,16,128,128]{3,2,1,0:T(8,128)(2,1)}, u32[]{:S(2)}) copy-start(bf16[1,16,128,128]{3,2,1,0:T(8,128)(2,1)} %param.10) | copy-start | bytes 1572868
  7.2 52.3 %reduce-scatter.2.cloned.1.call-start = ((), (), s32[]{:S(2)}) async-start(), calls=%async_computation.1 | async-start | bytes 655360 | tf_op jit(solution)/shard_map/reduce_scatter | solution.py:65
  7.2 11.1 %collective-permute-start = (bf16[128,512]{1,0:T(8,128)(2,1)}, bf16[128,512]{1,0:T(8,128)(2,1)S(1)}, u32[]{:S(2)}, u32[]{:S(2)}) collective-permute-start(bf16[128,512]{1,0:T(8,128)(2,1)} %bitcast.78), channel_id=1, source_target_pairs={{0,16},{8,24},{1,17},{9,25},{2,18},{10,26},{3,19},{11,27},{4,20},{... | collective-permute-start | bytes 393224 | tf_op jit(solution)/shard_map/ppermute | solution.py:30
  12.2 6.2 %collective-permute-start.1 = (bf16[128,512]{1,0:T(8,128)(2,1)}, bf16[128,512]{1,0:T(8,128)(2,1)S(1)}, u32[]{:S(2)}, u32[]{:S(2)}) collective-permute-start(bf16[128,512]{1,0:T(8,128)(2,1)} %bitcast.79), channel_id=1, source_target_pairs={{0,8},{8,16},{16,24},{1,9},{9,17},{17,25},{2,10},{10,18},{18,26},{... | collective-permute-start | bytes 393224 | tf_op jit(solution)/shard_map/ppermute | solution.py:30
  15.7 7.1 %collective-permute-start.2 = (bf16[128,512]{1,0:T(8,128)(2,1)}, bf16[128,512]{1,0:T(8,128)(2,1)S(1)}, u32[]{:S(2)}, u32[]{:S(2)}) collective-permute-start(bf16[128,512]{1,0:T(8,128)(2,1)} %bitcast.80), channel_id=1, source_target_pairs={{8,0},{16,8},{24,16},{9,1},{17,9},{25,17},{10,2},{18,10},{26,18},{... | collective-permute-start | bytes 393224 | tf_op jit(solution)/shard_map/ppermute | solution.py:30
  27.1 5.5 %copy-start.3 = (s32[1,16]{1,0:T(1,128)S(1)}, s32[1,16]{1,0:T(1,128)}, u32[]{:S(2)}) copy-start(s32[1,16]{1,0:T(1,128)} %param.11) | copy-start | bytes 196
  32.7 26.8 %copy-start.1 = (bf16[512,512]{1,0:T(8,128)(2,1)S(1)}, bf16[512,512]{1,0:T(8,128)(2,1)}, u32[]{:S(2)}) copy-start(bf16[512,512]{1,0:T(8,128)(2,1)} %param.9) | copy-start | bytes 1572868
  37.0 23.7 %copy-start.5 = (bf16[1,128,512]{2,1,0:T(8,128)(2,1)S(1)}, bf16[1,128,512]{2,1,0:T(8,128)(2,1)}, u32[]{:S(2)}) copy-start(bf16[1,128,512]{2,1,0:T(8,128)(2,1)} %param.8) | copy-start | bytes 393220
  37.9 156.9 %all-reduce.2.cloned.1.call-start = ((), (), s32[]{:S(2)}) async-start(), calls=%async_computation.2 | async-start | bytes 2097152 | tf_op jit(solution)/shard_map/psum | solution.py:79
  59.4 5.5 %copy-start.2 = (bf16[128,512]{1,0:T(8,128)(2,1)S(1)}, bf16[128,512]{1,0:T(8,128)(2,1)}, u32[]{:S(2)}) copy-start(bf16[128,512]{1,0:T(8,128)(2,1)} %reduce-scatter.2.cloned.1.call-done) | copy-start | bytes 393220
  61.0 6.9 %collective-permute-start.3 = (bf16[128,512]{1,0:T(8,128)(2,1)S(1)}, bf16[128,512]{1,0:T(8,128)(2,1)S(1)}, u32[]{:S(2)}, u32[]{:S(2)}) collective-permute-start(bf16[128,512]{1,0:T(8,128)(2,1)S(1)} %get-tuple-element.8), channel_id=1, source_target_pairs={{0,2},{2,4},{4,6},{6,0},{1,3},{3,5},{5,7},{7,1},{8,10},{10,12},{12... | collective-permute-start | bytes 393224 | tf_op jit(solution)/shard_map/ppermute | solution.py:17
  61.1 6.9 %collective-permute-start.4 = (bf16[128,512]{1,0:T(8,128)(2,1)S(1)}, bf16[128,512]{1,0:T(8,128)(2,1)S(1)}, u32[]{:S(2)}, u32[]{:S(2)}) collective-permute-start(bf16[128,512]{1,0:T(8,128)(2,1)S(1)} %get-tuple-element.8), channel_id=1, source_target_pairs={{0,6},{2,0},{4,2},{6,4},{1,7},{3,1},{5,3},{7,5},{8,14},{10,8},{12,... | collective-permute-start | bytes 393224 | tf_op jit(solution)/shard_map/ppermute | solution.py:20
  68.0 7.5 %collective-permute-start.5 = (bf16[128,512]{1,0:T(8,128)(2,1)S(1)}, bf16[128,512]{1,0:T(8,128)(2,1)S(1)}, u32[]{:S(2)}, u32[]{:S(2)}) collective-permute-start(bf16[128,512]{1,0:T(8,128)(2,1)S(1)} %collective-permute-done.3), channel_id=1, source_target_pairs={{0,2},{2,4},{4,6},{6,0},{1,3},{3,5},{5,7},{7,1},{8,10},{10,12},{12... | collective-permute-start | bytes 393224 | tf_op jit(solution)/shard_map/ppermute | solution.py:17
  78.9 5.5 %copy-start.4 = (s32[1,16]{1,0:T(1,128)S(1)}, s32[1,16]{1,0:T(1,128)}, u32[]{:S(2)}) copy-start(s32[1,16]{1,0:T(1,128)} %param.12) | copy-start | bytes 196
  89.5 8.0 %collective-permute-start.6 = (bf16[128,512]{1,0:T(8,128)(2,1)S(1)}, bf16[128,512]{1,0:T(8,128)(2,1)S(1)}, u32[]{:S(2)}, u32[]{:S(2)}) collective-permute-start(bf16[128,512]{1,0:T(8,128)(2,1)S(1)} %bitcast.75), channel_id=1, source_target_pairs={{16,0},{24,8},{17,1},{25,9},{18,2},{26,10},{19,3},{27,11},{20,4},{... | collective-permute-start | bytes 393224 | tf_op jit(solution)/shard_map/ppermute | solution.py:30
  90.8 6.9 %collective-permute-start.7 = (bf16[128,512]{1,0:T(8,128)(2,1)S(1)}, bf16[128,512]{1,0:T(8,128)(2,1)S(1)}, u32[]{:S(2)}, u32[]{:S(2)}) collective-permute-start(bf16[128,512]{1,0:T(8,128)(2,1)S(1)} %bitcast.76), channel_id=1, source_target_pairs={{8,0},{16,8},{24,16},{9,1},{17,9},{25,17},{10,2},{18,10},{26,18},{... | collective-permute-start | bytes 393224 | tf_op jit(solution)/shard_map/ppermute | solution.py:30
  92.2 7.7 %collective-permute-start.8 = (bf16[128,512]{1,0:T(8,128)(2,1)S(1)}, bf16[128,512]{1,0:T(8,128)(2,1)S(1)}, u32[]{:S(2)}, u32[]{:S(2)}) collective-permute-start(bf16[128,512]{1,0:T(8,128)(2,1)S(1)} %bitcast.77), channel_id=1, source_target_pairs={{0,8},{8,16},{16,24},{1,9},{9,17},{17,25},{2,10},{10,18},{18,26},{... | collective-permute-start | bytes 393224 | tf_op jit(solution)/shard_map/ppermute | solution.py:30
Sparse Core Ops, SparseCore 0:
  38.0 21.3 reduce-scatter.1
  66.4 128.3 all-reduce.1
